TPU v7x, 32 devices: a whole 2x2x4 slice. The times are simulated.
32 devices in a mesh: dp: 16 (over z, y, core), branch: 2 (over x).
Axes of the slice: x: 2, y: 2, z: 4, core: 2. Of those that a mesh axis runs over, the one named last changes fastest.
Arguments:
- tokens: bfloat16 [8192, 512], P(('dp', 'branch')), may hold values from -6 to 6
- wavlm: bfloat16 [8192, 1024], P('dp'), may hold values from -6 to 6
- cotangent: bfloat16 [8192, 512], P(('dp', 'branch')), may hold values from -6 to 6
- lengths: int32 [32, 4], P(('dp', 'branch')), may hold values from 1 to 128, 256 in all within a row
- codes: int32 [8192, 8], P('dp'), may hold values from 0 to 2047
- enc_qkv: bfloat16 [512, 1536], replicated, may hold values from -0.25 to 0.25
- enc_out: bfloat16 [512, 512], replicated, may hold values from -1 to 1
- enc_up: bfloat16 [512, 2048], replicated, may hold values from -0.25 to 0.25
- enc_down: bfloat16 [2048, 512], replicated, may hold values from -0.125 to 0.125
- dec_qkv: bfloat16 [512, 1536], replicated, may hold values from -0.25 to 0.25
- dec_out: bfloat16 [512, 512], replicated, may hold values from -1 to 1
- dec_up: bfloat16 [512, 2048], replicated, may hold values from -0.25 to 0.25
- dec_down: bfloat16 [2048, 512], replicated, may hold values from -0.125 to 0.125
- vectors: float32 [2, 4, 512], replicated, may hold values from 0.25 to 1.75
- proj_in: bfloat16 [2, 512, 256], P('branch'), may hold values from -0.25 to 0.25
- proj_out: bfloat16 [2, 256, 512], P('branch'), may hold values from -0.375 to 0.375
- codebooks: bfloat16 [8, 2048, 256], replicated, may hold values from -6 to 6
- distill_proj: bfloat16 [256, 1024], replicated, may hold values from -0.375 to 0.375
Outputs:
- decoded: bfloat16 [8192, 512], P(('dp', 'branch'))
- input_grad: float32 [8192, 512], P(('dp', 'branch'))
- enc_qkv_grad: float32 [786432], P(('dp', 'branch'))
- enc_out_grad: float32 [262144], P(('dp', 'branch'))
- enc_up_grad: float32 [1048576], P(('dp', 'branch'))
- enc_down_grad: float32 [1048576], P(('dp', 'branch'))
- dec_qkv_grad: float32 [786432], P(('dp', 'branch'))
- dec_out_grad: float32 [262144], P(('dp', 'branch'))
- dec_up_grad: float32 [1048576], P(('dp', 'branch'))
- dec_down_grad: float32 [1048576], P(('dp', 'branch'))
- vectors_grad: float32 [4096], P(('dp', 'branch'))
- proj_in_grad: float32 [262144], P(('dp', 'branch'))
- proj_out_grad: float32 [262144], P(('dp', 'branch'))
- codebooks_grad: float32 [4194304], P(('dp', 'branch'))
- distill_grad: float32 [262144], P(('dp', 'branch'))
Inputs may be any that keep to these rules, and one draw needn't show every extreme that they name: `lengths`: each row holds the frame counts of the clips packed on one device, in order; they sum to 256, and the longest clip of each row has 128 frames.
All inputs are finite; a program needn't handle non-finite values.
Results may differ from a plain program's by a relative error of at most 0.025.
Values may be sent and summed in bfloat16 or wider, within the bound.
A program may use at most 192 MiB of HBM per device.

v0:
```python
import functools
import math

import jax
import jax.numpy as jnp
from jax import lax
from jax.experimental import pallas as pl
from jax.experimental.pallas import tpu as pltpu
from jax.sharding import PartitionSpec as P

HEADS = 8
WINDOW = 250
EPS_NORM = 1e-05
EPS_COS = 1e-06
BETA = 0.25
DISTILL = 10.0
ROPE_BASE = 10000.0

MESH = pl.DeviceIdType.MESH
F32 = jnp.float32
BF16 = jnp.bfloat16
TILE = 512
PAIR = 128
HALF = 256


def dot(left, right):
    return lax.dot_general(left, right, (((1,), (0,)), ((), ())), preferred_element_type=F32)


def dot_t(left, right):
    return lax.dot_general(left, right, (((1,), (1,)), ((), ())), preferred_element_type=F32)


def t_dot(left, right):
    return lax.dot_general(left, right, (((0,), (0,)), ((), ())), preferred_element_type=F32)


def iota(shape, dim):
    return lax.broadcasted_iota(jnp.int32, shape, dim)


def aligned(index, size):
    return pl.ds(pl.multiple_of(index * size, size), size)


class Refs(dict):
    __getattr__ = dict.__getitem__
    __setattr__ = dict.__setitem__


class Moves:
    def __init__(self, semaphores):
        self.semaphores, self.count = semaphores, 0

    def start(self, source, target):
        move = pltpu.make_async_copy(source, target, self.semaphores.at[self.count])
        self.count += 1
        move.start()
        return move


def layer_scratch(rows, width, ff):
    return Refs(
        x=pltpu.VMEM((rows, width), F32),
        s1=pltpu.VMEM((rows, 1), F32),
        h=pltpu.VMEM((rows, width), BF16),
        h1t=pltpu.VMEM((width, rows), BF16),
        h2t=pltpu.VMEM((width, rows), BF16),
        rinv=pltpu.VMEM((rows, width), F32),
        qkv=pltpu.VMEM((rows, 3 * width), BF16),
        mix=pltpu.VMEM((rows, width), BF16),
        ao=pltpu.VMEM((rows, width), F32),
        x2=pltpu.VMEM((rows, width), F32),
        s2=pltpu.VMEM((rows, 1), F32),
        act=pltpu.VMEM((rows, ff), BF16),
        dg=pltpu.VMEM((rows, ff), BF16),
        fo=pltpu.VMEM((rows, width), F32),
        grad=pltpu.VMEM((rows, width), BF16),
        gx=pltpu.VMEM((rows, width), F32),
        acc=pltpu.VMEM((rows, width), F32),
        wide=pltpu.VMEM((4, rows, HALF), F32),
        change=pltpu.VMEM((2, rows, rows), BF16),
        w_qkv_v=pltpu.VMEM((width, 3 * width), BF16),
        w_out_v=pltpu.VMEM((width, width), BF16),
        w_up_v=pltpu.VMEM((width, ff), BF16),
        w_down_v=pltpu.VMEM((ff, width), BF16),
    )


def shaped(shape, kind):
    return jax.ShapeDtypeStruct(shape, kind)


def frame_tables(r):
    rows = r.cos.shape[0]
    place = iota((rows, PAIR), 0)
    query, key = iota((rows, rows), 0), iota((rows, rows), 1)
    begin, begin_query = jnp.zeros_like(place), jnp.zeros_like(query)
    edge = 0
    for clip in range(r.lengths.shape[1] - 1):
        edge = edge + r.lengths[0, clip]
        begin = jnp.where(place >= edge, edge, begin)
        begin_query = jnp.where(query >= edge, edge, begin_query)
    allowed = (key >= begin_query) & (key <= query) & (query - key < WINDOW)
    r.bias[...] = jnp.where(allowed, 0.0, -1e30)
    lane = iota((rows, PAIR), 1)
    rate = jnp.exp((lane % 32).astype(F32) * (-math.log(ROPE_BASE) / 32))
    angle = (place - begin).astype(F32) * rate
    r.cos[...] = jnp.cos(angle)
    sine = jnp.sin(angle)
    r.sin[...] = jnp.where(lane % 64 < 32, -sine, sine)


def rotated(value, cosine, sine):
    lane = iota(value.shape, 1)
    swapped = jnp.where(lane % 64 < 32, pltpu.roll(value, PAIR - 32, 1), pltpu.roll(value, 32, 1))
    return value * cosine + swapped * sine


def head_masks(rows):
    low = iota((rows, PAIR), 1) < 64
    return (jnp.where(low, 1.0, 0.0).astype(BF16), jnp.where(low, 0.0, 1.0).astype(BF16))


def row_blocks(rows, step):
    return [slice(i, i + step) for i in range(0, rows, step)]


def attention_project(r, w_qkv, gain):
    rows, width = r.x.shape
    scale = gain(0)
    for at in row_blocks(rows, 64):
        x = r.x[at, :]
        s1 = lax.rsqrt(jnp.mean(x * x, axis=1, keepdims=True) + EPS_NORM)
        r.s1[at, :] = s1
        r.h[at, :] = (x * s1 * scale).astype(BF16)
    for half in range(3 * width // HALF):
        slot, part = half % 4, half // (width // HALF)
        cols = slice(half * HALF, (half + 1) * HALF)
        r.wide[slot] = dot(r.h[...], w_qkv[:, cols])
        for at in row_blocks(rows, 64):
            for p in range(HALF // PAIR):
                value = r.wide[slot, at, p * PAIR : (p + 1) * PAIR]
                if part < 2:
                    value = rotated(value, r.cos[at, :], r.sin[at, :])
                low = value.astype(BF16)
                if part == 0:
                    low = (low.astype(F32) * 0.125).astype(BF16)
                r.qkv[at, half * HALF + p * PAIR : half * HALF + (p + 1) * PAIR] = low
    r.h1t[...] = r.h[...].T


def attention_mix(r, w_out, gain):
    rows, width = r.x.shape
    masks = head_masks(rows)
    low = iota((rows, PAIR), 1) < 64
    pairs = width // PAIR
    for p in range(pairs):
        query = r.qkv[:, p * PAIR : (p + 1) * PAIR]
        key = r.qkv[:, (p + pairs) * PAIR : (p + pairs + 1) * PAIR]
        value = r.qkv[:, (p + 2 * pairs) * PAIR : (p + 2 * pairs + 1) * PAIR]
        outs = []
        for h in range(2):
            head = 2 * p + h
            slot = head % 4
            r.wide[slot] = dot_t(query * masks[h], key)
            for at in row_blocks(rows, 64):
                seen = PAIR if at.stop <= PAIR else rows
                scores = r.wide[slot, at, :seen] + r.bias[at, :seen]
                weights = jnp.exp(scores - jnp.max(scores, axis=1, keepdims=True))
                r.att[head, at, :seen] = weights.astype(BF16)
                if seen < rows:
                    r.att[head, at, seen:] = jnp.zeros((64, rows - seen), BF16)
            outs.append(dot(r.att[head], value * masks[h] + masks[1 - h]))
        inverse = 1.0 / pltpu.roll(jnp.where(low, outs[1], outs[0]), 64, 1)
        r.rinv[:, p * PAIR : (p + 1) * PAIR] = inverse
        r.mix[:, p * PAIR : (p + 1) * PAIR] = (jnp.where(low, outs[0], outs[1]) * inverse).astype(BF16)
    r.ao[...] = dot(r.mix[...], w_out[...])
    scale_one, scale_two = gain(1), gain(2)
    for at in row_blocks(rows, 64):
        x2 = r.x[at, :] + scale_one * r.ao[at, :]
        r.x2[at, :] = x2
        s2 = lax.rsqrt(jnp.mean(x2 * x2, axis=1, keepdims=True) + EPS_NORM)
        r.s2[at, :] = s2
        r.h[at, :] = (x2 * s2 * scale_two).astype(BF16)
    r.h2t[...] = r.h[...].T


def gelu_parts(pre):
    slope = math.sqrt(2.0 / math.pi)
    square = pre * pre
    bent = jnp.tanh(slope * pre * (1.0 + 0.044715 * square))
    half = 0.5 * (1.0 + bent)
    turn = 0.5 * pre * (1.0 - bent * bent) * slope * (1.0 + 3.0 * 0.044715 * square)
    return (pre * half).astype(BF16), half + turn


def ffn_forward(r, w_up, w_down):
    rows, ff = r.act.shape
    for half in range(ff // HALF):
        slot, cols = half % 4, slice(half * HALF, (half + 1) * HALF)
        r.wide[slot] = dot(r.h[...], w_up[:, cols])
        for at in row_blocks(rows, 32):
            act, slope = gelu_parts(r.wide[slot, at, :])
            r.act[at, cols] = act
            r.dg[at, cols] = slope.astype(BF16)
    r.fo[...] = dot(r.act[...], w_down[...])


def ffn_both(r, w_up, w_down, grad_up, grad_down, first, last):
    rows = r.act.shape[0]
    for t in range(first, last):
        cols = slice(t * TILE, (t + 1) * TILE)
        for side in range(TILE // HALF):
            part = slice(t * TILE + side * HALF, t * TILE + (side + 1) * HALF)
            r.wide[side] = dot(r.h[...], w_up[:, part])
            r.wide[2 + side] = dot_t(r.grad[...], w_down[part, :])
            for at in row_blocks(rows, 32):
                act, slope = gelu_parts(r.wide[side, at, :])
                r.act[at, part] = act
                r.dg[at, part] = (r.wide[2 + side, at, :] * slope).astype(BF16)
        grad_up.shift((t - first) * TILE).put(dot(r.h2t[...], r.dg[:, cols]))
        put_rows(grad_down, t_dot(r.act[:, cols], r.grad[...]), t)


def ffn_back_sum(r, w_up):
    r.acc[...] = dot_t(r.dg[...], w_up[...])


def norm_back(stream, inverse, grad):
    mean = jnp.mean(grad * stream, axis=1, keepdims=True)
    return inverse * grad - stream * (inverse * inverse * inverse * mean)


def column_sum(value):
    return jnp.sum(value, axis=0, keepdims=True)


class Place:
    def __init__(self, ref, col=0, chunk=None):
        self.ref, self.col, self.chunk = ref, col, chunk

    def shift(self, by):
        return Place(self.ref, self.col + by, self.chunk)

    def put(self, value):
        value = value.astype(BF16)
        cols = slice(self.col, self.col + value.shape[1])
        if self.chunk is None:
            self.ref[:, cols] = value
            return
        blocks, rows = self.ref.shape[:2]
        for owner in range(blocks):
            self.ref[self.chunk.index(owner), :, cols] = value[owner * rows : (owner + 1) * rows]


def put_rows(places, value, tile):
    value = value.astype(BF16)
    begin = 0
    for place in places:
        part = value[:, begin : begin + place.ref.shape[-1]]
        begin += place.ref.shape[-1]
        if place.chunk is None:
            place.ref[tile * TILE : tile * TILE + TILE, :] = part
            continue
        rows = place.ref.shape[1]
        for i in range(TILE // rows):
            place.ref[place.chunk.index(tile * (TILE // rows) + i)] = part[i * rows : (i + 1) * rows]


def ffn_backward_begin(r, gain, gy_ref):
    scale = gain(3)
    for at in row_blocks(r.grad.shape[0], 64):
        r.grad[at, :] = (scale * gy_ref[at, :].astype(F32)).astype(BF16)


def ffn_backward_tiles(r, w_down, grad_up, grad_down, first, last):
    rows = r.act.shape[0]
    for t in range(first, last):
        cols = slice(t * TILE, (t + 1) * TILE)
        for side in range(TILE // HALF):
            part = slice(t * TILE + side * HALF, t * TILE + (side + 1) * HALF)
            slot = (2 * t + side) % 4
            r.wide[slot] = dot_t(r.grad[...], w_down[part, :])
            for at in row_blocks(rows, 64):
                r.dg[at, part] = (r.wide[slot, at, :] * r.dg[at, part].astype(F32)).astype(BF16)
        put_rows(grad_down, t_dot(r.act[:, cols], r.grad[...]), t)
        grad_up.shift((t - first) * TILE).put(dot(r.h2t[...], r.dg[:, cols]))


def ffn_backward_end(r, gain, gy_ref, gain_out):
    scale = gain(2)
    to_gain = to_scale = 0.0
    for at in row_blocks(r.x2.shape[0], 32):
        gy = gy_ref[at, :].astype(F32)
        to_scale = to_scale + column_sum(gy * r.fo[at, :])
        back, x2, s2 = r.acc[at, :], r.x2[at, :], r.s2[at, :]
        to_gain = to_gain + column_sum(back * x2 * s2)
        r.gx[at, :] = gy + norm_back(x2, s2, back * scale)
    gain_out[3:4, :] = to_scale
    gain_out[2:3, :] = to_gain


def attention_backward_out(r, w_out, gain, grad_out, gain_out):
    scale = gain(1)
    to_scale = 0.0
    for at in row_blocks(r.gx.shape[0], 64):
        gx = r.gx[at, :]
        to_scale = to_scale + column_sum(gx * r.ao[at, :])
        r.grad[at, :] = (scale * gx).astype(BF16)
    gain_out[1:2, :] = to_scale
    grad_out.put(t_dot(r.mix[...], r.grad[...]))
    r.grad[...] = dot_t(r.grad[...], w_out[...]).astype(BF16)


def attention_backward_pairs(r, first, last):
    rows, width = r.x.shape
    masks = head_masks(rows)
    masks_t = [jnp.where((iota((PAIR, rows), 0) < 64) == (h == 0), 1.0, 0.0).astype(BF16) for h in range(2)]
    pairs = width // PAIR
    for p in range(first, last):
        lanes = [slice((p + i * pairs) * PAIR, (p + i * pairs + 1) * PAIR) for i in range(3)]
        query, key, value = (r.qkv[:, at] for at in lanes)
        grad_mixed = (r.grad[:, lanes[0]].astype(F32) * r.rinv[:, lanes[0]]).astype(BF16)
        product = (grad_mixed.astype(F32) * r.mix[:, lanes[0]].astype(F32)).astype(BF16)
        beside = jnp.concatenate([value, jnp.full(value.shape, -1.0, BF16)], axis=1)
        query_t, grad_t = query.T, grad_mixed.T
        to_query = to_key = to_value = 0.0
        for h in range(2):
            head = 2 * p + h
            slot = head % 4
            both = jnp.concatenate([grad_mixed * masks[h], product * masks[h]], axis=1)
            r.wide[slot] = dot_t(both, beside)
            for at in row_blocks(rows, 64):
                r.change[h, at, :] = (r.att[head, at, :].astype(F32) * r.wide[slot, at, :]).astype(BF16)
            to_query = to_query + dot(r.change[h], key * masks[h])
            to_key = to_key + dot(query_t * masks_t[h], r.change[h])
            to_value = to_value + dot(grad_t * masks_t[h], r.att[head])
        cosine, sine = r.cos[...], -r.sin[...]
        r.qkv[:, lanes[0]] = rotated(to_query * 0.125, cosine, sine).astype(BF16)
        r.qkv[:, lanes[1]] = rotated(to_key.T, cosine, sine).astype(BF16)
        r.qkv[:, lanes[2]] = to_value.T.astype(BF16)


def attention_backward_in(r, grad_qkv, part):
    width = r.x.shape[1]
    grad_qkv.put(dot(r.h1t[...], r.qkv[:, part * width : (part + 1) * width]))


def attention_backward_end(r, w_qkv, gain, gain_out):
    r.acc[...] = dot_t(r.qkv[...], w_qkv[...])
    scale = gain(0)
    to_gain = 0.0
    for at in row_blocks(r.x.shape[0], 32):
        back, x, s1 = r.acc[at, :], r.x[at, :], r.s1[at, :]
        to_gain = to_gain + column_sum(back * x * s1)
        r.gx[at, :] = r.gx[at, :] + norm_back(x, s1, back * scale)
    gain_out[0:1, :] = to_gain


class Segment:
    def __init__(self, result, base, stride, col, blocks, row, rows):
        self.result, self.base, self.stride, self.col, self.blocks = result, base, stride, col, blocks
        self.row, self.rows = row, rows


class Chunk:
    def __init__(self, rows, columns, order, segments):
        self.rows, self.columns, self.order, self.segments = rows, columns, order, segments

    def index(self, owner):
        bits = len(self.order)
        return sum((owner >> (bits - 1 - dim) & 1) << (bits - 1 - stage) for stage, dim in enumerate(self.order))

    def shape(self, leading):
        return (2**leading, self.rows, self.columns)

    def bytes(self, bits):
        return 2**bits * self.rows * self.columns * 2


def plan(chunks, work, bits, book_bytes):
    core, x, y = bits - 2, bits - 1, bits - 3
    ends, middle = -1, -2
    free, pending, done = {}, [], []
    now = 0.0

    def carry(link, size, rate=42e3):
        free[link] = max(now, free.get(link, 0.0)) + size / rate
        return free[link]

    def begin(name, stage):
        if name == BOOKS:
            size = 1.2 * 2 ** (bits - 3) * book_bytes
            if stage == 0:
                there = max(carry(y, size), carry(ends, 1.5 * size), carry(middle, 2 * size))
            else:
                there = carry(core, 4 * book_bytes, 400e3) if stage == 1 else carry(x, 2 * book_bytes)
        else:
            dim = chunks[name].order[stage]
            size = chunks[name].bytes(bits) / 2 ** (stage + 1)
            if dim == core:
                there = carry(core, size, 400e3)
            elif dim == x or dim == y:
                there = carry(dim, size)
            else:
                there = carry(ends, size)
                if dim < y - 1:
                    there = max(there, carry(middle, 2 * size))
        pending.append((there + 1.5, name, stage))

    def finish(limit):
        nonlocal now
        acts = []
        while pending:
            pending.sort(key=lambda p: p[0])
            if pending[0][0] + (0.5 if limit < math.inf else 0.0) > limit:
                break
            at, name, stage = pending.pop(0)
            if name == BOOKS:
                cost = (6.0, 0.6, 0.3)[stage]
            else:
                cost = 0.25 + 0.3e-6 * chunks[name].bytes(bits) / 2 ** (stage + 1)
            now = max(now, at) + cost
            limit = max(limit, now)
            acts.append((name, stage))
            if stage + 1 < (3 if name == BOOKS else bits):
                begin(name, stage + 1)
        return acts

    for took, _, names in work:
        now += 0.95 * took
        for name in names:
            begin(name, 0)
        done.append(finish(now))
    done.append(finish(math.inf))
    return done


def store_segment(packed, first, segment, value):
    for i in range(segment.blocks):
        where = pl.ds(first + segment.base + i, segment.rows, stride=segment.stride)
        packed[where, :] = value[
            segment.row : segment.row + segment.rows, segment.col + i * 128 : segment.col + (i + 1) * 128
        ]


class Halving:
    def __init__(self, chunks, bits, recv, packed, first, send_sem, recv_sem):
        self.chunks = chunks
        self.bits, self.recv, self.packed, self.first = bits, recv, packed, first
        self.send_sem, self.recv_sem = send_sem, recv_sem
        self.copies = {}
        dp, branch = lax.axis_index("dp"), lax.axis_index("branch")
        self.mine, self.partner = [], []
        for dim in range(bits - 1):
            weight = 2 ** (bits - 2 - dim)
            bit = dp // weight % 2
            self.mine.append(bit)
            self.partner.append({"dp": dp + weight * (1 - 2 * bit), "branch": branch})
        self.mine.append(branch)
        self.partner.append({"dp": dp, "branch": 1 - branch})

    def near_level(self, other):
        dp = lax.axis_index("dp")
        for i in range(self.bits - 2):
            if other >> i & 1:
                dp = dp + 2 ** (i + 1) * (1 - 2 * self.mine[self.bits - 3 - i])
        return {"dp": dp, "branch": lax.axis_index("branch")}

    def barrier(self):
        semaphore = pltpu.get_barrier_semaphore()
        levels = 2 ** (self.bits - 2)
        targets = self.partner[self.bits - 2 :] + [self.near_level(other) for other in range(1, levels)]
        for target in targets:
            pl.semaphore_signal(semaphore, inc=1, device_id=target, device_id_type=MESH)
        return lambda: pl.semaphore_wait(semaphore, len(targets))

    def half(self, ref, name, stage, other):
        mine = self.mine[self.chunks[name].order[stage]]
        count = 2 ** (self.bits - 1 - stage)
        return ref.at[pl.ds((1 - mine if other else mine) * count, count)]

    def remote(self, source, target, device, *key):
        slot = len(self.copies)
        self.copies[key] = pltpu.make_async_remote_copy(
            src_ref=source,
            dst_ref=target,
            send_sem=self.send_sem.at[slot],
            recv_sem=self.recv_sem.at[slot],
            device_id=device,
            device_id_type=MESH,
        )
        self.copies[key].start()

    def send(self, name, stage, source):
        dim = self.chunks[name].order[stage]
        self.remote(source, self.recv[name][stage], self.partner[dim], name, stage)

    def send_half(self, name, stage, ref):
        self.send(name, stage, self.half(ref, name, stage, True))

    def arrived(self, *key):
        self.copies[key].wait_recv()

    def add(self, name, stage, own):
        chunk = self.chunks[name]
        got = self.recv[name][stage]
        if stage == self.bits - 1:
            value = own[0].astype(F32) + got[0].astype(F32)
            for segment in chunk.segments:
                store_segment(self.packed, self.first[segment.result], segment, value)
            return
        count = 2 ** (self.bits - 1 - stage)
        step = min(count, 4)

        def some(i, carry):
            at = pl.ds(i * step, step)
            got[at] = got[at] + own[at]
            return carry

        lax.fori_loop(0, count // step, some, 0)

    def finish(self, name, stage, before):
        self.arrived(name, stage)
        self.add(name, stage, self.half(before, name, stage, False))
        if stage + 1 < self.bits:
            self.send_half(name, stage + 1, self.recv[name][stage])

    def drain(self):
        for copy in self.copies.values():
            copy.wait_send()


BOOKS = "books"


def quantizer_semantic(r):
    sem_code = r.chosen[0]
    rows, code_width = sem_code.shape
    columns = [slice(i * HALF, (i + 1) * HALF) for i in range(r.distill_v.shape[1] // HALF)]
    for i, cols in enumerate(columns):
        r.wide[i] = dot(sem_code, r.distill_v[:, cols])

    def row_sum(parts):
        return jnp.sum(sum(parts), axis=1, keepdims=True)

    for at in row_blocks(rows, 32):
        prediction = [r.wide[i, at, :] for i in range(len(columns))]
        target = [r.wavlm_v[at, cols].astype(F32) for cols in columns]
        pred_norm = lax.rsqrt(row_sum([p * p for p in prediction]) + EPS_COS)
        target_norm = lax.rsqrt(row_sum([w * w for w in target]) + EPS_COS)
        cosine = row_sum([p * w for p, w in zip(prediction, target)]) * (pred_norm * target_norm)
        from_target = -DISTILL * pred_norm * target_norm
        from_prediction = DISTILL * cosine * pred_norm * pred_norm
        for p, w, cols in zip(prediction, target, columns):
            r.act[at, cols] = (w * from_target + p * from_prediction).astype(BF16)
    grad_pred = r.act[:, : r.distill_v.shape[1]]
    put_distill(r.places.distill, dot(sem_code.T, grad_pred))
    r.gy[:, :code_width] = dot_t(grad_pred, r.distill_v[...])


def quantizer_latent(r):
    levels, rows, code_width = r.chosen.shape
    latent_t = r.latent[...].T
    r.wide[0] = dot_t(r.gquant[...], r.pout_v[0])
    r.wide[1] = dot(r.latent[...], r.pin_v[0])
    r.wide[2] = dot_t(r.gquant[...], r.pout_v[1])
    r.wide[3] = dot(r.latent[...], r.pin_v[1])
    put_group(r.places.pout, 0, t_dot(r.chosen[0], r.gquant[...]))
    put_group(r.places.pout, 1, t_dot(r.ac[...], r.gquant[...]))
    for at in row_blocks(rows, 32):
        grad_sem = r.wide[0, at, :] + r.gy[at, :code_width]
        commit = 2.0 * BETA * (r.wide[1, at, :] - r.chosen[0, at, :].astype(F32))
        r.g_rows[0, at, :] = (grad_sem - commit).astype(BF16)
        r.grad[at, :code_width] = (grad_sem + commit).astype(BF16)
        grad_ac, residual = r.wide[2, at, :], r.wide[3, at, :]
        for level in range(1, levels):
            residual = residual - r.chosen[level, at, :].astype(F32)
        carry = jnp.zeros_like(residual)
        for level in range(levels - 1, 0, -1):
            carry = carry + 2.0 * BETA * residual
            r.g_rows[level, at, :] = (grad_ac - carry).astype(BF16)
            residual = residual + r.chosen[level, at, :].astype(F32)
        r.grad[at, code_width:] = (grad_ac + carry).astype(BF16)
    put_group(r.places.pin, 0, dot(latent_t, r.grad[:, :code_width]))
    put_group(r.places.pin, 1, dot(latent_t, r.grad[:, code_width:]))
    r.gy[...] = dot_t(r.grad[...], jnp.concatenate([r.pin_v[0], r.pin_v[1]], axis=1))


def put_group(place, group, value):
    target, total = place.ref, value.shape[0]
    value = value.astype(BF16)
    if place.chunk is None:
        target[group * total : (group + 1) * total, :] = value
        return
    blocks, height, columns = target.shape[0] // 2, target.shape[1], value.shape[1]
    for i in range(blocks):
        for part in range(total // blocks // height):
            first = i * (total // blocks) + part * height
            cols = slice(place.col + part * columns, place.col + (part + 1) * columns)
            target[place.chunk.index(group * blocks + i), :, cols] = value[first : first + height]


def put_distill(place, value):
    target = place.ref
    if place.chunk is None:
        target[...] = value.astype(BF16)
        return
    blocks, height = target.shape[:2]
    rows = value.shape[0] // blocks
    columns = value.shape[1] * rows // height
    for i in range(blocks):
        part = value[i * rows : (i + 1) * rows]
        part = jnp.concatenate([part[:, at : at + columns] for at in range(0, value.shape[1], columns)], axis=0)
        target[place.chunk.index(i), :, place.col : place.col + columns] = part.astype(BF16)


def one_hot_rows(codes, first, count):
    row = iota((count, codes.shape[1]), 0)
    return jnp.where(codes - first == row, 1.0, 0.0).astype(BF16)


def pick_codes(r):
    levels, _, entries, code_width = r.books.shape
    entries = entries * r.books.shape[1]
    rows = r.cos.shape[0]
    slots = r.ring.shape[0]
    branch = lax.axis_index("branch")
    own = r.codes[:, pl.ds(pl.multiple_of(branch * rows, rows), rows)]
    r.code_rows[...] = jnp.broadcast_to(own[:, None, :], r.code_rows.shape)
    columns = jnp.concatenate([own.astype(F32), jnp.zeros((PAIR - levels, rows), F32)], axis=0).T
    lane = iota(columns.shape, 1)
    entry = iota((rows, entries), 1)
    r.code_cols[...] = columns
    r.ac_sum[...] = jnp.zeros(r.ac_sum.shape, F32)

    def book(level):
        slot = level % slots
        return pltpu.make_async_copy(r.books.at[level], r.ring.at[slot], r.sem_book.at[slot])

    def pick(level, carry):
        code = jnp.sum(jnp.where(lane == level, r.code_cols[...], 0.0), axis=1, keepdims=True)
        one_hot = jnp.where(entry == code.astype(jnp.int32), 1.0, 0.0).astype(BF16)
        book(level).wait()
        got = dot(one_hot, r.ring[level % slots].reshape(entries, code_width))
        r.chosen[level] = got.astype(BF16)
        r.ac_sum[...] += jnp.where(level > 0, got, 0.0)

        @pl.when(level + slots < levels)
        def _():
            book(level + slots).start()

        return carry

    def begin():
        for level in range(slots):
            book(level).start()

    def run():
        lax.fori_loop(0, levels, pick, 0, unroll=4)
        r.ac[...] = r.ac_sum[...].astype(BF16)

    return begin, run


def step_kernel(chunks, first_rows, bits, ins, outs, scratch):
    r = Refs({**ins, **outs, **scratch})
    t = r.t = Refs(r.t)
    r.att, r.g_rows, r.g_got, r.book_own = (r.ring.at[i] for i in range(4))
    r.ac_sum, r.code_cols = r.acc.at[:, : r.ac.shape[1]], r.gx.at[:, :PAIR]
    branch = lax.axis_index("branch")
    rows, width = r.tokens.shape
    levels, parts, entries, code_width = r.books.shape
    entries = entries * parts
    tiles = r.w_up_v.shape[1] // TILE
    pairs = width // PAIR
    if chunks:
        sums = Halving(chunks, bits, r.recv, r.packed, first_rows, r.send_sem, r.recv_sem)
        mine, level = sums.mine[bits - 2], lax.axis_index("dp") // 2
        wait_barrier = sums.barrier()
    moves = Moves(r.sem_move)
    begin_pick, run_pick = pick_codes(r)
    begin_pick()
    got_pout = [moves.start(r.pout_own.at[0], r.pout_v.at[branch])]
    if chunks:
        wait_barrier()
        sums.remote(r.pout_own.at[0], r.pout_v.at[branch], sums.partner[bits - 1], POUT)
    else:
        got_pout.append(moves.start(r.pout_other.at[0], r.pout_v.at[1 - branch]))
    got_rest = [
        moves.start(r.distill, r.distill_v),
        moves.start(r.wavlm.at[pl.ds(pl.multiple_of(branch * rows, rows), rows)], r.wavlm_v),
    ]
    got_attention, got_ffn, got_cotangent, got_pin, got_tokens, got_attention_two = ([] for _ in range(6))
    frame_tables(r)

    def fetch_rest():
        got_attention.extend([moves.start(r.dec_qkv, r.w_qkv_v), moves.start(r.dec_out, r.w_out_v)])
        got_ffn.extend([moves.start(r.dec_up, r.w_up_v), moves.start(r.dec_down, r.w_down_v)])
        got_cotangent.append(moves.start(r.cotangent, r.cotangent_v))
        got_pin.append(moves.start(r.pin_own.at[0], r.pin_v.at[branch]))
        if not chunks:
            got_pin.append(moves.start(r.pin_other.at[0], r.pin_v.at[1 - branch]))
        got_tokens.append(moves.start(r.tokens, r.tokens_v))
        got_attention_two.extend([moves.start(r.enc_qkv, r.w_qkv_e), moves.start(r.enc_out, r.w_out_e)])

    if chunks:
        def at(name, col=0):
            return Place(t[name], col, chunks[name])

        dec_down, enc_down = [at(DD0), at(DD1)], [at(ED0), at(ED1), at(ED2)]
        place = r.places = Refs(
            dec_up=[at(DU0), at(DU1)],
            dec_out=at(DA0),
            dec_qkv=[at(DA0, width), at(DA1), at(DA2)],
            enc_up=[at(EU0), at(EU1)],
            enc_out=at(EA0),
            enc_qkv=[at(EA1), at(EA2), at(EA3)],
            distill=at(DISTILL_GRAD),
            pout=at(MISC),
            pin=at(MISC, width),
        )
    else:
        dec_down, enc_down = [Place(t.dec_down)], [Place(t.enc_down)]
        place = r.places = Refs(
            dec_up=[Place(t.dec_up, i * tiles // 2 * TILE) for i in range(2)],
            dec_out=Place(t.dec_out),
            dec_qkv=[Place(t.dec_qkv, i * width) for i in range(3)],
            enc_up=[Place(t.enc_up, i * tiles // 2 * TILE) for i in range(2)],
            enc_out=Place(t.enc_out),
            enc_qkv=[Place(t.enc_qkv, i * width) for i in range(3)],
            distill=Place(t.distill),
            pout=Place(t.pout),
            pin=Place(t.pin),
        )

    def wait(moves, other=None):
        for move in moves:
            move.wait()
        if chunks and other is not None:
            sums.arrived(other)

    def layer_value(target, gain):
        for at in row_blocks(rows, 64):
            target[at, :] = (r.x2[at, :] + gain(3) * r.fo[at, :]).astype(BF16)

    def dec_gain(i):
        return r.vectors[1, i : i + 1, :]

    def enc_gain(i):
        return r.vectors[0, i : i + 1, :]

    def pick():
        run_pick()
        fetch_rest()

    def semantic():
        wait(got_rest)
        quantizer_semantic(r)

    def quant():
        wait(got_pout, POUT)
        if chunks:
            sums.remote(r.pin_own.at[0], r.pin_v.at[branch], sums.partner[bits - 1], PIN)
        r.x[...] = dot(jnp.concatenate([r.chosen[0], r.ac[...]], axis=1), r.pout_v[...].reshape(-1, width))
        if chunks:
            for other in range(1, levels):
                target = sums.near_level(other)
                sums.remote(r.code_rows.at[target_level(target)], r.code_got.at[other], target, CODES, other)
            r.code_got[0] = r.code_rows[level]

    def target_level(target):
        return next(iter(target.values())) // 2

    def dec_project():
        wait(got_attention)
        attention_project(r, r.w_qkv_v, dec_gain)

    def dec_mix():
        attention_mix(r, r.w_out_v, dec_gain)

    def dec_ffn(half):
        def run():
            if half == 0:
                wait(got_ffn)
                wait(got_cotangent)
                ffn_backward_begin(r, dec_gain, r.cotangent_v)
            first, last = half * tiles // 2, (half + 1) * tiles // 2
            ffn_both(r, r.w_up_v, r.w_down_v, place.dec_up[half], dec_down, first, last)

        return run

    def dec_ffn_end():
        r.fo[...] = dot(r.act[...], r.w_down_v[...])
        layer_value(r.decoded, dec_gain)
        ffn_back_sum(r, r.w_up_v)
        ffn_backward_end(r, dec_gain, r.cotangent_v, r.dec_gains)
        got_ffn[:] = [moves.start(r.enc_up, r.w_up_v), moves.start(r.enc_down, r.w_down_v)]

    def dec_out():
        attention_backward_out(r, r.w_out_v, dec_gain, place.dec_out, r.dec_gains)

    def attention_pairs(first, last):
        return lambda: attention_backward_pairs(r, first, last)

    def dec_in(part):
        def run():
            attention_backward_in(r, place.dec_qkv[part], part)
            if part == 2:
                attention_backward_end(r, r.w_qkv_v, dec_gain, r.dec_gains)
                r.gquant[...] = r.gx[...].astype(BF16)

        return run

    def enc_project():
        wait(got_tokens)
        r.x[...] = r.tokens_v[...].astype(F32)
        wait(got_attention_two)
        attention_project(r, r.w_qkv_e, enc_gain)

    def enc_mix():
        attention_mix(r, r.w_out_e, enc_gain)

    def enc_ffn():
        wait(got_ffn)
        ffn_forward(r, r.w_up_v, r.w_down_v)
        layer_value(r.latent, enc_gain)

    def quantizer():
        wait(got_pin, PIN)
        quantizer_latent(r)
        if chunks:
            for other in reversed(range(1, levels)):
                target = sums.near_level(other)
                sums.arrived(CODES, other)
                sums.remote(r.g_rows.at[target_level(target)], r.g_got.at[other], target, BOOKS, 0, other)
            r.g_got[0] = r.g_rows[level]

    def book_half(core, put):
        quarter = entries // 4
        for side in range(2):
            r.book_sum[...] = jnp.zeros_like(r.book_sum)
            first = (core * 2 + side) * quarter

            def add(source, carry):
                one_hot = one_hot_rows(r.code_got[source, 0:1, :], first, quarter)
                r.book_sum[...] += dot(one_hot, r.g_got[source])
                return carry

            lax.fori_loop(0, levels, add, 0, unroll=4)
            put(side, r.book_sum[...])

    def finish_books(stage):
        blocks = entries // 4 // rows
        other_core, other_side = sums.partner[bits - 2], sums.partner[bits - 1]
        if stage == 0:
            for other in range(1, levels):
                sums.arrived(BOOKS, 0, other)

            def put(side, value):
                r.book_send[side] = value.astype(BF16)

            def keep(side, value):
                r.book_own[side * blocks : (side + 1) * blocks] = value.astype(BF16).reshape((blocks, rows, code_width))

            book_half(1 - mine, put)
            sums.remote(r.book_send, r.book_got, other_core, BOOKS, 1)
            book_half(mine, keep)
        elif stage == 1:
            sums.arrived(BOOKS, 1)
            for side in range(2):
                own = r.book_own[side * blocks : (side + 1) * blocks]
                r.book_got[side] = r.book_got[side] + own.reshape(r.book_got.shape[1:])
            sums.remote(r.book_got.at[1 - branch], r.book_last, other_side, BOOKS, 2)
        else:
            sums.arrived(BOOKS, 2)
            total = r.book_got[branch].astype(F32) + r.book_last[...].astype(F32)
            blocks = code_width // 128
            store_segment(r.packed, first_rows[BOOKS], Segment(BOOKS, 0, blocks, 0, blocks, 0, entries // 4), total)

    def all_books():
        parts = entries // TILE

        def one(step, carry):
            at = step // parts
            one_hot = one_hot_rows(r.code_rows[at, 0:1, :], step % parts * TILE, TILE)
            t.books[at, aligned(step % parts, TILE), :] = dot(one_hot, r.g_rows[at]).astype(BF16)
            return carry

        lax.fori_loop(0, levels * parts, one, 0)

    def enc_ffn_back(half):
        def run():
            first, last = half * tiles // 2, (half + 1) * tiles // 2
            if half == 0:
                ffn_backward_begin(r, enc_gain, r.gy)
            ffn_backward_tiles(r, r.w_down_v, place.enc_up[half], enc_down, first, last)
            if half == 1:
                ffn_back_sum(r, r.w_up_v)
                ffn_backward_end(r, enc_gain, r.gy, r.gains)

        return run

    def enc_out():
        attention_backward_out(r, r.w_out_e, enc_gain, place.enc_out, r.gains)

    def enc_in(part):
        def run():
            attention_backward_in(r, place.enc_qkv[part], part)
            if part == 2:
                attention_backward_end(r, r.w_qkv_e, enc_gain, r.gains)
                r.grad_tokens[...] = r.gx[...]
                if chunks:
                    spread_gains()

        return run

    def spread_gains():
        last, height = chunks[EA3], t.ea3.shape[1]
        for layer, ref in enumerate((r.gains, r.dec_gains)):
            for row in range(4):
                for block in range(width // 128):
                    owner = (layer * 4 + row) * (width // 128) + block
                    value = jnp.broadcast_to(ref[row : row + 1, block * 128 : (block + 1) * 128], (height, 128))
                    t.ea3[last.index(owner), :, width : width + 128] = value.astype(BF16)

    work = [
        (6.5, pick, ()),
        (2.0, semantic, (DISTILL_GRAD,)),
        (0.7, quant, ()),
        (1.5, dec_project, ()),
        (2.5, dec_mix, ()),
        (2.6, dec_ffn(0), (DU0,)),
        (2.0, dec_ffn(1), (DD0, DD1, DU1)),
        (0.7, dec_ffn_end, ()),
        (1.2, dec_out, ()),
        (1.6, attention_pairs(0, pairs // 2), ()),
        (1.6, attention_pairs(pairs // 2, pairs), ()),
        (0.6, dec_in(0), (DA0,)),
        (0.6, dec_in(1), (DA1,)),
        (0.8, dec_in(2), (DA2,)),
        (1.5, enc_project, ()),
        (2.5, enc_mix, ()),
        (2.2, enc_ffn, ()),
        (2.0, quantizer, (BOOKS, MISC)),
        (2.0, enc_ffn_back(0), (EU0,)),
        (2.0, enc_ffn_back(1), (EU1, ED0, ED1, ED2)),
        (1.2, enc_out, (EA0,)),
        (1.6, attention_pairs(0, pairs // 2), ()),
        (1.6, attention_pairs(pairs // 2, pairs), ()),
        (0.6, enc_in(0), (EA1,)),
        (0.6, enc_in(1), (EA2,)),
        (1.0, enc_in(2), (EA3,)),
    ]
    if not chunks:
        for _, run, _ in work:
            run()
            if run is quantizer:
                all_books()
        return
    actions = plan(chunks, work, bits, rows * code_width * 2)

    def finish(name, stage):
        if name == BOOKS:
            finish_books(stage)
        else:
            sums.finish(name, stage, r.recv[name][stage - 1] if stage else t[name])

    for (_, run, made), acts in zip(work, actions):
        run()
        for name in made:
            if name != BOOKS:
                sums.send_half(name, 0, t[name])
        for name, stage in acts:
            finish(name, stage)
    for name, stage in actions[-1]:
        finish(name, stage)
    sums.drain()


POUT, PIN, CODES = 1, 2, 3
DISTILL_GRAD = "di"
DD0, DD1, DU0, DU1, DA0, DA1, DA2, MISC = "dd0", "dd1", "du0", "du1", "da0", "da1", "da2", "misc"
EU0, EU1, ED0, ED1, ED2 = "eu0", "eu1", "ed0", "ed1", "ed2"
EA0, EA1, EA2, EA3 = "ea0", "ea1", "ea2", "ea3"


def step(given, devices, with_sums):
    rows, width = given.tokens.shape
    ff = given.enc_up.shape[1]
    levels, entries, code_width = given.books.shape
    given.books = given.books.reshape(levels, -1, rows, code_width)
    bits = devices.bit_length() - 1
    vmem, hbm = pl.BlockSpec(memory_space=pltpu.VMEM), pl.BlockSpec(memory_space=pl.ANY)
    scratch = layer_scratch(rows, width, ff)
    scratch.update(
        w_qkv_e=pltpu.VMEM((width, 3 * width), BF16),
        w_out_e=pltpu.VMEM((width, width), BF16),
        cos=pltpu.VMEM((rows, PAIR), F32),
        sin=pltpu.VMEM((rows, PAIR), F32),
        bias=pltpu.VMEM((rows, rows), F32),
        ring=pltpu.VMEM((4,) + given.books.shape[1:], BF16),
        code_rows=pltpu.VMEM((levels, 8, rows), jnp.int32),
        chosen=pltpu.VMEM((levels, rows, code_width), BF16),
        ac=pltpu.VMEM((rows, code_width), BF16),
        gquant=pltpu.VMEM((rows, width), BF16),
        gy=pltpu.VMEM((rows, width), F32),
        latent=pltpu.VMEM((rows, width), BF16),
        pin_v=pltpu.VMEM((2, width, code_width), BF16),
        pout_v=pltpu.VMEM((2, code_width, width), BF16),
        distill_v=pltpu.VMEM(given.distill.shape, BF16),
        wavlm_v=pltpu.VMEM((rows, given.wavlm.shape[1]), BF16),
        tokens_v=pltpu.VMEM((rows, width), BF16),
        cotangent_v=pltpu.VMEM((rows, width), BF16),
        sem_move=pltpu.SemaphoreType.DMA((14,)),
        sem_book=pltpu.SemaphoreType.DMA((4,)),
    )
    outs = Refs(decoded=shaped((rows, width), BF16), grad_tokens=shaped((rows, width), F32))
    chunks, first_rows = {}, {}
    params = dict(vmem_limit_bytes=60 * 2**20)
    if with_sums:
        params.update(collective_id=0, has_side_effects=True)
        c, x, y = bits - 2, bits - 1, bits - 3
        b, a = range(y)
        share = width // devices
        low, high = ff // devices, share
        wide, half, blocks = ff // 128, ff // 256, width // 128
        third, quarter = 3 * blocks, blocks // 4
        chunks = dict(
            di=Chunk(
                high,
                width,
                [c, y, x, a, b],
                [
                    Segment(8, 0, 2 * blocks, 0, blocks, 0, high // 2),
                    Segment(8, blocks, 2 * blocks, 0, blocks, high // 2, high // 2),
                ],
            ),
            du0=Chunk(high, ff // 2, [c, y, a, x, b], [Segment(2, 0, wide, 0, half, 0, high)]),
            dd0=Chunk(low, width // 2, [c, a, y, b, x], [Segment(3, 0, blocks, 0, 2 * quarter, 0, low)]),
            dd1=Chunk(low, width // 2, [c, y, x, a, b], [Segment(3, 2 * quarter, blocks, 0, 2 * quarter, 0, low)]),
            du1=Chunk(high, ff // 2, [c, x, y, a, b], [Segment(2, half, wide, 0, half, 0, high)]),
            da0=Chunk(
                high,
                2 * width,
                [c, x, y, a, b],
                [Segment(1, 0, blocks, 0, blocks, 0, high), Segment(0, 0, third, width, blocks, 0, high)],
            ),
            da1=Chunk(high, width, [c, a, x, y, b], [Segment(0, blocks, third, 0, blocks, 0, high)]),
            da2=Chunk(high, width, [c, y, x, a, b], [Segment(0, 2 * blocks, third, 0, blocks, 0, high)]),
            misc=Chunk(
                high,
                2 * width,
                [c, x, y, a, b],
                [
                    Segment(9, 0, blocks, 0, blocks, 0, high),
                    Segment(10, 0, blocks // 2, width, blocks // 2, 0, high),
                    Segment(10, high * blocks // 2, blocks // 2, width + code_width, blocks // 2, 0, high),
                ],
            ),
            eu0=Chunk(high, ff // 2, [c, x, a, y, b], [Segment(6, 0, wide, 0, half, 0, high)]),
            eu1=Chunk(high, ff // 2, [c, x, y, a, b], [Segment(6, half, wide, 0, half, 0, high)]),
            ed0=Chunk(low, width // 2, [c, x, y, a, b], [Segment(7, 0, blocks, 0, 2 * quarter, 0, low)]),
            ed1=Chunk(low, width // 4, [c, y, x, a, b], [Segment(7, 2 * quarter, blocks, 0, quarter, 0, low)]),
            ed2=Chunk(low, width // 4, [c, y, a, b, x], [Segment(7, 3 * quarter, blocks, 0, quarter, 0, low)]),
            ea0=Chunk(high, width, [c, x, y, a, b], [Segment(5, 0, blocks, 0, blocks, 0, high)]),
            ea1=Chunk(high, width, [c, y, x, a, b], [Segment(4, 0, third, 0, blocks, 0, high)]),
            ea2=Chunk(high, width, [c, x, a, y, b], [Segment(4, blocks, third, 0, blocks, 0, high)]),
            ea3=Chunk(
                high,
                width + 128,
                [c, x, y, a, b],
                [Segment(4, 2 * blocks, third, 0, blocks, 0, high), Segment(11, 0, 1, width, 1, 0, 8)],
            ),
        )
        rows_of = [high * 3 * blocks, high * blocks, high * wide, low * blocks] * 2
        rows_of += [high * blocks, high * blocks, high * blocks, 8, entries // 4 * code_width // 128]
        first_rows = {i: sum(rows_of[:i]) for i in range(len(rows_of))}
        first_rows[BOOKS] = first_rows[len(rows_of) - 1]
        copies = len(chunks) * bits + 2 * levels + 2
        scratch.update(
            t={name: pltpu.VMEM(c.shape(bits), BF16) for name, c in chunks.items()},
            recv={
                name: [pltpu.VMEM(c.shape(bits - 1 - stage), BF16) for stage in range(bits)]
                for name, c in chunks.items()
            },
            gains=pltpu.VMEM((4, width), F32),
            dec_gains=pltpu.VMEM((4, width), F32),
            code_got=pltpu.VMEM((levels, 8, rows), jnp.int32),
                book_sum=pltpu.VMEM((entries // 4, code_width), F32),
            book_send=pltpu.VMEM((2, entries // 4, code_width), BF16),
            book_got=pltpu.VMEM((2, entries // 4, code_width), BF16),
            book_last=pltpu.VMEM((entries // 4, code_width), BF16),
            send_sem=pltpu.SemaphoreType.DMA((copies,)),
            recv_sem=pltpu.SemaphoreType.DMA((copies,)),
        )
        outs.packed = shaped((sum(rows_of), 128), F32)
    else:
        outs.update(gains=shaped((4, width), F32), dec_gains=shaped((4, width), F32))
        outs.t = dict(
            enc_qkv=shaped(given.enc_qkv.shape, BF16),
            enc_out=shaped(given.enc_out.shape, BF16),
            enc_up=shaped(given.enc_up.shape, BF16),
            enc_down=shaped(given.enc_down.shape, BF16),
            dec_qkv=shaped(given.enc_qkv.shape, BF16),
            dec_out=shaped(given.enc_out.shape, BF16),
            dec_up=shaped(given.enc_up.shape, BF16),
            dec_down=shaped(given.enc_down.shape, BF16),
            pin=shaped((2 * width, code_width), BF16),
            pout=shaped((2 * code_width, width), BF16),
            books=shaped((levels, entries, code_width), BF16),
            distill=shaped(given.distill.shape, BF16),
        )
    in_specs = dict.fromkeys(given, hbm)
    in_specs.update(
        lengths=pl.BlockSpec(memory_space=pltpu.SMEM), codes=vmem, vectors=vmem
    )
    got = pl.pallas_call(
        functools.partial(step_kernel, chunks, first_rows, bits),
        out_shape={k: pltpu.VMEM(v.shape, v.dtype) for k, v in outs.items()} if with_sums else dict(outs),
        in_specs=[in_specs],
        out_specs=jax.tree.map(lambda _: vmem, dict(outs)),
        scratch_shapes=[dict(scratch)],
        compiler_params=pltpu.CompilerParams(**params),
        name="step",
    )(dict(given))
    got = Refs(got)
    if not with_sums:
        return got
    last = [shaped((rows, 128), F32) for rows in rows_of]
    last[11] = shaped((1, 128), F32)

    def hand_on(packed, decoded, grad, *refs):
        outs, moves = refs[:-1], Moves(refs[-1])
        parts = [packed.at[pl.ds(first_rows[i], ref.shape[0])] for i, ref in enumerate(outs[:-2])]
        leaving = [moves.start(part, ref) for part, ref in zip(parts + [decoded, grad], outs)]
        for move in leaving:
            move.wait()

    return pl.pallas_call(
        hand_on,
        out_shape=last + [outs.decoded, outs.grad_tokens],
        in_specs=[vmem] * 3,
        out_specs=[hbm] * (len(last) + 2),
        scratch_shapes=[pltpu.SemaphoreType.DMA((len(last) + 2,))],
        compiler_params=pltpu.CompilerParams(vmem_limit_bytes=16 * 2**20),
        name="results",
    )(got.packed, got.decoded, got.grad_tokens)


def body(
    tokens,
    wavlm,
    cotangent,
    lengths,
    codes,
    enc_qkv,
    enc_out,
    enc_up,
    enc_down,
    dec_qkv,
    dec_out,
    dec_up,
    dec_down,
    vectors,
    proj_in,
    proj_out,
    codebooks,
    distill_proj,
):
    width = tokens.shape[1]
    devices = lax.axis_size("dp") * lax.axis_size("branch")
    with_sums = devices == 4 * codebooks.shape[0] and width // devices % 16 == 0
    given = Refs(
        tokens=tokens,
        wavlm=wavlm,
        cotangent=cotangent,
        lengths=lengths,
        codes=codes.T,
        enc_qkv=enc_qkv,
        enc_out=enc_out,
        enc_up=enc_up,
        enc_down=enc_down,
        dec_qkv=dec_qkv,
        dec_out=dec_out,
        dec_up=dec_up,
        dec_down=dec_down,
        vectors=vectors,
        pin_own=proj_in,
        pout_own=proj_out,
        books=codebooks,
        distill=distill_proj,
    )
    if with_sums:
        *sums, decoded, grad_tokens = step(given, devices, True)
        sums = [part.reshape(-1) for part in sums]
        order = (4, 5, 6, 7, 0, 1, 2, 3, 11, 10, 9, 12, 8)
        return (decoded, grad_tokens, *[sums[i] for i in order])
    swap = [(0, 1), (1, 0)]
    given.pin_other = lax.ppermute(proj_in, "branch", swap)
    given.pout_other = lax.ppermute(proj_out, "branch", swap)
    s = step(given, devices, False)
    t = Refs(s.t)
    gains = jnp.concatenate([s.gains, s.dec_gains])
    local = [t.enc_qkv, t.enc_out, t.enc_up, t.enc_down, t.dec_qkv, t.dec_out, t.dec_up, t.dec_down]
    local += [gains, t.pin, t.pout, t.books, t.distill]
    sums = [
        lax.psum_scatter(part.astype(F32).reshape(-1), ("dp", "branch"), scatter_dimension=0, tiled=True)
        for part in local
    ]
    return (s.decoded, s.grad_tokens, *sums)


def solution(mesh):
    rows, whole = P(("dp", "branch"), None), P()
    placed = (rows, P("dp", None), rows, rows, P("dp", None)) + (whole,) * 9
    placed += (P("branch", None, None),) * 2 + (whole,) * 2
    return jax.shard_map(
        body,
        mesh=mesh,
        in_specs=placed,
        out_specs=(rows, rows) + (P(("dp", "branch")),) * 13,
        check_vma=False,
    )
```

profile of v0, /device:TPU:0, one launch (start us, length us, event | category | flops | bytes accessed | tf_op | source)
XLA Modules:
  0.0 95.1 jit_solution(2171535553943136756)
XLA Ops:
  0.7 92.8 %step.1 = (bf16[256,512]{1,0:T(8,128)(2,1)S(1)}, f32[256,512]{1,0:T(8,128)S(1)}, f32[2760,128]{1,0:T(8,128)S(1)}) custom-call(bf16[8,8,256,256]{3,2,1,0:T(8,128)(2,1)} %bitcast.15, s32[8,512]{1,0:T(8,128)} %bitcast.16, bf16[256,512]{1,0:T(8,128)(2,1)} %ins__cotangent__.1, bf16[2048,512]{1,0:T(8,128)(2,1)} %ins__dec_down__.1, ...), custom_call_target="tpu_custom_call" | custom-call | tf_op jit(solution)/shard_map/step/pallas_call | solution.py:1120
  93.5 1.5 %results.1 = (f32[192,128]{1,0:T(8,128)}, f32[64,128]{1,0:T(8,128)}, f32[256,128]{1,0:T(8,128)}, f32[256,128]{1,0:T(8,128)}, f32[192,128]{1,0:T(8,128)}, /*index...) custom-call(f32[2760,128]{1,0:T(8,128)S(1)} %get-tuple-element.33.pa, ...), custom_call_target="tpu_custom_call" | custom-call | tf_op jit(solution)/shard_map/results/pallas_call | solution.py:1142
where the time goes:
time: 95.4 us; the launch traced here: 95.1 us
  Pallas kernels  94.3 us (99%)
    pallas_call x1, Pallas kernels, step(): pl.pallas_call(functools.partial(step_kernel, chunks, first_rows, bits),...  92.8 us

commit v1 on v0

--- a/solution.py
+++ b/solution.py
@@ -736,11 +736,15 @@
             pin=Place(t.pin),
         )
 
-    def wait(moves, other=None):
+    def core_rows(ref):
+        half = ref.shape[0] // 2
+        return ref.at[pl.ds(pl.multiple_of(mine * half, half), half)]
+
+    def wait(moves, *other):
         for move in moves:
             move.wait()
-        if chunks and other is not None:
-            sums.arrived(other)
+        if chunks and other:
+            sums.arrived(*other)
 
     def layer_value(target, gain):
         for at in row_blocks(rows, 64):
@@ -763,7 +767,7 @@
     def quant():
         wait(got_pout, POUT)
         if chunks:
-            sums.remote(r.pin_own.at[0], r.pin_v.at[branch], sums.partner[bits - 1], PIN)
+            sums.remote(core_rows(r.pin_own.at[0]), core_rows(r.pin_v.at[branch]), sums.partner[bits - 1], PIN)
         r.x[...] = dot(jnp.concatenate([r.chosen[0], r.ac[...]], axis=1), r.pout_v[...].reshape(-1, width))
         if chunks:
             for other in range(1, levels):
@@ -800,6 +804,10 @@
         got_ffn[:] = [moves.start(r.enc_up, r.w_up_v), moves.start(r.enc_down, r.w_down_v)]
 
     def dec_out():
+        if chunks:
+            sums.arrived(PIN)
+            there = core_rows(r.pin_v.at[1 - branch])
+            sums.remote(there, there, sums.partner[bits - 2], PIN, 1)
         attention_backward_out(r, r.w_out_v, dec_gain, place.dec_out, r.dec_gains)
 
     def attention_pairs(first, last):
@@ -829,7 +837,7 @@
         layer_value(r.latent, enc_gain)
 
     def quantizer():
-        wait(got_pin, PIN)
+        wait(got_pin, PIN, 1)
         quantizer_latent(r)
         if chunks:
             for other in reversed(range(1, levels)):
@@ -897,11 +905,12 @@
             if half == 0:
                 ffn_backward_begin(r, enc_gain, r.gy)
             ffn_backward_tiles(r, r.w_down_v, place.enc_up[half], enc_down, first, last)
-            if half == 1:
-                ffn_back_sum(r, r.w_up_v)
-                ffn_backward_end(r, enc_gain, r.gy, r.gains)
 
         return run
+
+    def enc_ffn_back_end():
+        ffn_back_sum(r, r.w_up_v)
+        ffn_backward_end(r, enc_gain, r.gy, r.gains)
 
     def enc_out():
         attention_backward_out(r, r.w_out_e, enc_gain, place.enc_out, r.gains)
@@ -946,7 +955,8 @@
         (2.2, enc_ffn, ()),
         (2.0, quantizer, (BOOKS, MISC)),
         (2.0, enc_ffn_back(0), (EU0,)),
-        (2.0, enc_ffn_back(1), (EU1, ED0, ED1, ED2)),
+        (1.6, enc_ffn_back(1), (EU1, ED0, ED1, ED2)),
+        (0.4, enc_ffn_back_end, ()),
         (1.2, enc_out, (EA0,)),
         (1.6, attention_pairs(0, pairs // 2), ()),
         (1.6, attention_pairs(pairs // 2, pairs), ()),
@@ -1079,7 +1089,7 @@
         rows_of += [high * blocks, high * blocks, high * blocks, 8, entries // 4 * code_width // 128]
         first_rows = {i: sum(rows_of[:i]) for i in range(len(rows_of))}
         first_rows[BOOKS] = first_rows[len(rows_of) - 1]
-        copies = len(chunks) * bits + 2 * levels + 2
+        copies = len(chunks) * bits + 2 * levels + 3
         scratch.update(
             t={name: pltpu.VMEM(c.shape(bits), BF16) for name, c in chunks.items()},
             recv={

time: 95.4 us -> 95.2 us (level)
  no operation moved by 1% of the time
where the time goes in v1:
time: 95.2 us; the launch traced here: 94.9 us
  Pallas kernels  94.1 us (99%)
    pallas_call x1, Pallas kernels, step(): pl.pallas_call(functools.partial(step_kernel, chunks, first_rows, bits),...  92.6 us

profile of v1, /device:TPU:0, one launch (start us, length us, event | category | flops | bytes accessed | tf_op | source)
XLA Modules:
  0.0 94.9 jit_solution(2227234979242601870)
XLA Ops:
  0.7 92.6 %step.1 = (bf16[256,512]{1,0:T(8,128)(2,1)S(1)}, f32[256,512]{1,0:T(8,128)S(1)}, f32[2760,128]{1,0:T(8,128)S(1)}) custom-call(bf16[8,8,256,256]{3,2,1,0:T(8,128)(2,1)} %bitcast.15, s32[8,512]{1,0:T(8,128)} %bitcast.16, bf16[256,512]{1,0:T(8,128)(2,1)} %ins__cotangent__.1, bf16[2048,512]{1,0:T(8,128)(2,1)} %ins__dec_down__.1, ...), custom_call_target="tpu_custom_call" | custom-call | tf_op jit(solution)/shard_map/step/pallas_call | solution.py:1130
  93.3 1.5 %results.1 = (f32[192,128]{1,0:T(8,128)}, f32[64,128]{1,0:T(8,128)}, f32[256,128]{1,0:T(8,128)}, f32[256,128]{1,0:T(8,128)}, f32[192,128]{1,0:T(8,128)}, /*index...) custom-call(f32[2760,128]{1,0:T(8,128)S(1)} %get-tuple-element.33.pa, ...), custom_call_target="tpu_custom_call" | custom-call | tf_op jit(solution)/shard_map/results/pallas_call | solution.py:1152
